TPU v7x, 32 devices: a whole 2x2x4 slice. The times are simulated.
32 devices in a mesh: layer: 2 (over y), tok: 4 (over z), task: 4 (over x, core).
Axes of the slice: x: 2, y: 2, z: 4, core: 2. Of those that a mesh axis runs over, the one named last changes fastest.
Arguments:
- activations: bfloat16 [56, 56, 1024], P('tok', 'layer', 'task'), parts along dimension 1
- counts: int32 [56, 1024], P(('layer', 'tok'), 'task'), parts along dimension 0, may hold values from 28 to 56
- candidates: int32 [56, 2], P('layer'), parts along dimension 0, may hold values from 0 to 27, as said below
Outputs:
- correlation: bfloat16 [28, 4, 1024, 1024], P('tok', 'layer', 'task'), parts along dimension 1
There are 2 independent parts, one for each index of `layer`. A program takes and returns all parts, laid end to end along the dimension named above; each array names one. Nothing has to cross between parts.
Inputs may be any that keep to these rules, and one draw needn't show every extreme that they name: `candidates`: row blocks b with equal b // 7 form one owner's 7 * 2 pairs; of their column blocks at most 4 have any one value of c // 7, and some value has exactly 4.
All inputs are finite; a program needn't handle non-finite values.
Results may differ from a plain program's by a relative error of at most 0.0057.
Values may be sent and summed in bfloat16 or wider, within the bound.
A program may use at most 64 MiB of HBM per device.

v0:
```python
import jax
import jax.numpy as jnp
from jax import lax
from jax.sharding import PartitionSpec as P


def normalize(values, counts):
    token_ids = jnp.arange(values.shape[0], dtype=jnp.int32)[:, None, None]
    live_mask = (token_ids < counts[None]).astype(jnp.float32)
    count_f = counts.astype(jnp.float32)
    widened = values.astype(jnp.float32)
    unit_mean = jnp.sum(widened * live_mask, axis=0) / count_f
    centered = (widened - unit_mean) * live_mask
    variance = jnp.sum(centered * centered, axis=0) / count_f
    return (centered * lax.rsqrt(variance + 1e-05) * lax.rsqrt(count_f)).astype(jnp.bfloat16)


def body(activations, counts, candidates):
    tok_count = lax.axis_size("tok")
    task_count = lax.axis_size("task")
    owned_raw = lax.all_to_all(activations, "tok", split_axis=1, concat_axis=0, tiled=True)
    scaled = normalize(owned_raw, counts)
    blocks_per = scaled.shape[1]
    slice_width = scaled.shape[2]
    full_width = slice_width * task_count
    cand_count = candidates.shape[1]
    per_owner = blocks_per * cand_count
    capacity = (per_owner + tok_count - 1) // tok_count
    wanted = candidates.reshape(tok_count, per_owner)
    source = wanted // blocks_per
    within_block = wanted % blocks_per
    order_ids = jnp.arange(per_owner, dtype=jnp.int32)
    earlier = order_ids[None, :] < order_ids[:, None]
    same_source = source[:, :, None] == source[:, None, :]
    rank_in = jnp.sum((same_source & earlier[None]).astype(jnp.int32), axis=2)
    my_index = lax.axis_index("tok")
    slot_ids = jnp.arange(capacity, dtype=jnp.int32)
    matched = (
        (source == my_index)[:, :, None] & (rank_in[:, :, None] == slot_ids[None, None, :])
    ).astype(jnp.int32)
    picked = jnp.sum(matched * within_block[:, :, None], axis=1).reshape(-1)
    filled = jnp.sum(matched, axis=1).reshape(-1)
    send_buffer = jnp.where(
        (filled > 0)[None, :, None], jnp.take(scaled, picked, axis=1), jnp.zeros((), jnp.bfloat16)
    )
    received = lax.all_to_all(send_buffer, "tok", split_axis=1, concat_axis=1, tiled=True)
    my_source = lax.dynamic_index_in_dim(source, my_index, 0, keepdims=False)
    my_rank = lax.dynamic_index_in_dim(rank_in, my_index, 0, keepdims=False)
    columns = jnp.take(received, my_source * capacity + my_rank, axis=1)
    rows_pair = jnp.repeat(scaled, cand_count, axis=1)
    tile_set = jnp.einsum(
        "tps,tpc->psc",
        rows_pair,
        lax.all_gather(columns, "task", axis=2, tiled=True),
        preferred_element_type=jnp.float32,
    ).astype(jnp.bfloat16)
    return tile_set.reshape(blocks_per, cand_count, slice_width, full_width)


def solution(mesh):
    return jax.shard_map(
        body,
        mesh=mesh,
        in_specs=(P("tok", "layer", "task"), P(("layer", "tok"), "task"), P("layer", None)),
        out_specs=P("tok", "layer", "task", None),
        check_vma=False,
    )
```

profile of v0, /device:TPU:0, one launch (start us, length us, event | category | flops | bytes accessed | tf_op | source)
XLA Modules:
  0.0 74.2 jit_solution(14821161539002427087)
XLA Ops:
  6.5 0.0 copy-start
  6.5 1.8 %copy.44 = bf16[14,28,256]{2,0,1:T(8,128)(2,1)} copy(bf16[14,28,256]{2,1,0:T(8,128)(2,1)} %param.3) | data formatting | bytes 401408 | tf_op args[0]
  8.3 6.3 %all-to-all-start = ((bf16[14,28,256]{2,0,1:T(8,128)(2,1)}), bf16[14,28,256]{2,0,1:T(8,128)(2,1)S(1)}, u32[]{:S(2)}, u32[]{:S(2)}) async-start(bf16[14,28,256]{2,0,1:T(8,128)(2,1)} %copy.44), calls=%async_computation | async-start | bytes 458752 | tf_op jit(solution)/shard_map/all_to_all | solution.py:21
  14.6 0.7 sign_compare_fusion
  15.3 0.7 broadcast_remainder_fusion
  16.0 0.1 copy.46
  16.1 0.1 ne.56
  16.2 0.1 copy.47
  16.3 0.1 rem.33
  16.4 0.1 copy.48
  16.5 0.1 div.29
  16.6 0.1 copy.49
  16.7 0.4 convert_reduce_fusion
  17.1 0.1 copy.50
  17.2 0.2 convert_reduce_fusion.1
  17.4 0.1 reshape.182
  17.5 0.1 reshape.181
  17.6 0.1 gt.11
  17.7 5.1 %all-to-all-done = bf16[14,28,256]{2,0,1:T(8,128)(2,1)S(1)} async-done(((bf16[14,28,256]{2,0,1:T(8,128)(2,1)}), bf16[14,28,256]{2,0,1:T(8,128)(2,1)S(1)}, u32[]{:S(2)}, u32[]{:S(2)}) %all-to-all-start) | async-done | bytes 200736 | tf_op jit(solution)/shard_map/all_to_all | solution.py:21
  22.9 0.0 copy-done
  22.9 0.1 fusion
  23.0 0.2 fusion.2
  23.3 0.1 reshape.184
  23.3 0.1 multiply_convert_fusion
  23.4 0.6 gather_fusion
  24.0 0.9 %select_bitcast_fusion = bf16[56,16,256]{2,0,1:T(8,128)(2,1)} fusion(bf16[16,56,256]{2,1,0:T(8,128)(2,1)S(1)} %gather_fusion, pred[16]{0:T(512)(128)(4,1)S(1)} %gt.11, pred[16]{0:T(512)(128)(4,1)S(1)} %compare_and_fusion), kind=kLoop, calls=%fused_computation.9 | loop fusion | flops 458752 | bytes 917536 | tf_op jit(solution)/shard_map/jit(_where)/select_n | solution.py:43
  24.9 3.5 %all-to-all-start.1 = ((bf16[56,16,256]{2,0,1:T(8,128)(2,1)}), bf16[56,16,256]{2,0,1:T(8,128)(2,1)S(1)}, u32[]{:S(2)}, u32[]{:S(2)}) async-start(bf16[56,16,256]{2,0,1:T(8,128)(2,1)} %select_bitcast_fusion), calls=%async_computation.1 | async-start | bytes 917504 | tf_op jit(solution)/shard_map/all_to_all | solution.py:46
  28.4 0.0 all-gather.2.cloned.1.call-start
  28.5 11.5 %all-to-all-done.1 = bf16[56,16,256]{2,0,1:T(8,128)(2,1)S(1)} async-done(((bf16[56,16,256]{2,0,1:T(8,128)(2,1)}), bf16[56,16,256]{2,0,1:T(8,128)(2,1)S(1)}, u32[]{:S(2)}, u32[]{:S(2)}) %all-to-all-start.1) | async-done | bytes 458784 | tf_op jit(solution)/shard_map/all_to_all | solution.py:46
  40.0 0.6 gather_fusion.1
  40.6 0.9 %select_bitcast_fusion.1 = bf16[56,14,256]{2,0,1:T(8,128)(2,1)} fusion(bf16[14,56,256]{2,1,0:T(8,128)(2,1)S(1)} %gather_fusion.1, pred[14]{0:T(512)(128)(4,1)S(1)} %get-tuple-element.7), kind=kLoop, calls=%fused_computation.10 | loop fusion | flops 200704 | bytes 802830 | tf_op jit(solution)/shard_map/jit(_take)/select_n | solution.py:49
  41.4 0.0 all-gather.2.cloned.1.call-update
  41.5 19.3 %all-gather.2.cloned.1.call-done = bf16[56,14,1024]{2,0,1:T(8,128)(2,1)} async-done(((bf16[56,14,256]{2,0,1:T(8,128)(2,1)}), bf16[56,14,1024]{2,0,1:T(8,128)(2,1)}) %all-gather.2.cloned.1.call-update) | async-done | bytes 1605648 | tf_op jit(solution)/shard_map/all_gather | solution.py:54
  60.8 6.6 %convolution_convert_fusion = bf16[14,256,1024]{2,1,0:T(8,128)(2,1)} fusion(bf16[56,14,256]{2,0,1:T(8,128)(2,1)S(1)} %bitcast.29, bf16[56,14,1024]{2,0,1:T(8,128)(2,1)} %all-gather.2.cloned.1.call-done), kind=kOutput, calls=%fused_computation.2 | convolution fusion | flops 414711808 | bytes 9347072 | tf_op jit(solution)/shard_map/tps,tpc->psc/dot_general | solution.py:51
  (16 shorter events, 0.2 us)
Async XLA Ops:
  6.5 16.3 %copy-start = (s32[7,256]{1,0:T(8,128)S(1)}, s32[7,256]{1,0:T(8,128)}, u32[]{:S(2)}) copy-start(s32[7,256]{1,0:T(8,128)} %param.4) | copy-start | bytes 21508
  8.3 14.5 %all-to-all-start = ((bf16[14,28,256]{2,0,1:T(8,128)(2,1)}), bf16[14,28,256]{2,0,1:T(8,128)(2,1)S(1)}, u32[]{:S(2)}, u32[]{:S(2)}) async-start(bf16[14,28,256]{2,0,1:T(8,128)(2,1)} %copy.44), calls=%async_computation | async-start | bytes 458752 | tf_op jit(solution)/shard_map/all_to_all | solution.py:21
  24.9 15.1 %all-to-all-start.1 = ((bf16[56,16,256]{2,0,1:T(8,128)(2,1)}), bf16[56,16,256]{2,0,1:T(8,128)(2,1)S(1)}, u32[]{:S(2)}, u32[]{:S(2)}) async-start(bf16[56,16,256]{2,0,1:T(8,128)(2,1)} %select_bitcast_fusion), calls=%async_computation.1 | async-start | bytes 917504 | tf_op jit(solution)/shard_map/all_to_all | solution.py:46
  28.4 32.4 %all-gather.2.cloned.1.call-start = ((), (), s32[]{:S(2)}) async-start(), calls=%async_computation.2 | async-start | bytes 2007040 | tf_op jit(solution)/shard_map/all_gather | solution.py:54
Sparse Core Ops, SparseCore 0:
  41.6 19.1 all-gather.1
where the time goes:
time: 74.5 us; the launch traced here: 74.2 us
  waiting for transfers between devices  35.9 us (48%)
  between operations  13.5 us (18%)
  starting transfers between devices  9.82 us (13%)
  matrix products  6.59 us (9%)
  other arithmetic  4.28 us (6%)
  local copies, waits for them, and re-layouts  4.02 us (5%)
    all_gather x1, waiting for transfers between devices, body(): lax.all_gather(columns, 'task', axis=2, tiled=True)  19.3 us
    all_to_all x1, waiting for transfers between devices, body(): lax.all_to_all(send_buffer, 'tok', split_axis=1, concat_axis=1, tiled=True)  11.5 us
    dot_general x1, matrix products, body(): jnp.einsum('tps,tpc->psc', rows_pair, lax.all_gather(columns, 'task', axi...  6.59 us
    all_to_all x1, starting transfers between devices, body(): lax.all_to_all(activations, 'tok', split_axis=1, concat_axis=0, tiled=True)  6.32 us
    all_to_all x1, waiting for transfers between devices, body(): lax.all_to_all(activations, 'tok', split_axis=1, concat_axis=0, tiled=True)  5.12 us
    all_to_all x1, starting transfers between devices, body(): lax.all_to_all(send_buffer, 'tok', split_axis=1, concat_axis=1, tiled=True)  3.47 us
    unnamed x3, local copies, waits for them, and re-layouts  1.76 us
  transfers between devices with their start and end apart: 3, of which 3 were waited for; matrix products, arithmetic and copies ran while one was open for 4% of the time, Pallas kernels for 0%

commit v1 on v0

--- a/solution.py
+++ b/solution.py
@@ -1,7 +1,14 @@
+import functools
+
 import jax
 import jax.numpy as jnp
 from jax import lax
+from jax.experimental import pallas as pl
+from jax.experimental.pallas import tpu as pltpu
 from jax.sharding import PartitionSpec as P
+
+MESH = pl.DeviceIdType.MESH
+ROWS = 16
 
 
 def normalize(values, counts):
@@ -57,9 +64,190 @@
     return tile_set.reshape(blocks_per, cand_count, slice_width, full_width)
 
 
+def flip(index, bit):
+    return index + bit - 2 * bit * ((index // bit) % 2)
+
+
+def exchange_kernel(tok_count, blocks_per, cand_count, act_ref, counts_ref, cand_ref, out_ref,
+                    padded, count_rows, select, sending, z_send, z_recv, x_send, x_recv,
+                    s_send, s_recv, r_send, r_recv):
+    me = lax.axis_index("tok")
+    task = lax.axis_index("task")
+    partner = flip(task, 2)
+    sibling = flip(task, 1)
+    pairs = blocks_per * cand_count
+    slots = pairs + blocks_per
+    tokens, blocks, width = act_ref.shape
+    rows, held = padded.shape[0], padded.shape[1]
+
+    def tok_peer(k):
+        other = me
+        if k & 1:
+            other = flip(other, 1)
+        if k & 2:
+            other = flip(other, 2)
+        return other
+
+    barrier = pltpu.get_barrier_semaphore()
+    for k in range(1, tok_count):
+        pl.semaphore_signal(barrier, inc=1, device_id={"tok": tok_peer(k)}, device_id_type=MESH)
+    for other in (partner, sibling):
+        pl.semaphore_signal(barrier, inc=1, device_id={"task": other}, device_id_type=MESH)
+
+    padded[...] = jnp.zeros_like(padded)
+    padded[0:tokens, 0:blocks, :] = act_ref[...]
+    count_rows[...] = jnp.zeros_like(count_rows)
+    counts = counts_ref[...]
+    for owner in range(tok_count):
+        mine = jnp.where(me == owner, counts, 0)
+        at = pl.ds(owner * blocks_per, blocks_per)
+        count_rows[0, at, :] = (mine // 16).astype(jnp.float32)
+        count_rows[1, at, :] = (mine % 16).astype(jnp.float32)
+    padded[tokens:tokens + 2] = count_rows[...].astype(jnp.bfloat16)
+    flat = padded[...].reshape(rows * held, width)
+    lane = lax.broadcasted_iota(jnp.int32, (rows, rows * held), 1)
+    row = lax.broadcasted_iota(jnp.int32, (rows, rows * held), 0)
+    offset = lane - held * row
+
+    def pick(owner):
+        for slot in range(slots):
+            if slot < pairs:
+                block = cand_ref[owner * blocks_per + slot // cand_count, slot % cand_count]
+            else:
+                block = owner * blocks_per + (slot - pairs)
+            select[slot] = jnp.where(offset == block, 1.0, 0.0).astype(jnp.bfloat16)
+        picked = jnp.dot(
+            select[...].reshape(slots * rows, rows * held), flat, preferred_element_type=jnp.float32
+        )
+        return picked.astype(jnp.bfloat16).reshape(slots, rows, width)
+
+    def z_copy(k):
+        return pltpu.make_async_remote_copy(
+            src_ref=sending.at[k], dst_ref=out_ref.at[task, me], send_sem=z_send.at[k],
+            recv_sem=z_recv.at[k], device_id={"tok": tok_peer(k)}, device_id_type=MESH)
+
+    def z_arrival(k):
+        return pltpu.make_async_remote_copy(
+            src_ref=sending.at[k], dst_ref=out_ref.at[task, tok_peer(k)], send_sem=z_send.at[k],
+            recv_sem=z_recv.at[k], device_id={"tok": tok_peer(k)}, device_id_type=MESH)
+
+    def task_copy(quarter, k, target, send, recv):
+        view = out_ref.at[quarter, tok_peer(k), 0:pairs]
+        return pltpu.make_async_remote_copy(
+            src_ref=view, dst_ref=view, send_sem=send.at[k],
+            recv_sem=recv.at[k], device_id={"task": target}, device_id_type=MESH)
+
+    order = [k for k in (2, 3, 1) if k < tok_count]
+    first = True
+    for k in order:
+        sending[k] = pick(tok_peer(k))
+        if first:
+            pl.semaphore_wait(barrier, tok_count + 1)
+            first = False
+        z_copy(k).start()
+    out_ref[task, me] = pick(me)
+
+    def pass_on(k):
+        task_copy(task, k, partner, x_send, x_recv).start()
+        task_copy(task, k, sibling, s_send, s_recv).start()
+
+    def relay(k):
+        task_copy(partner, k, partner, x_send, x_recv).wait_recv()
+        task_copy(partner, k, sibling, r_send, r_recv).start()
+
+    pass_on(0)
+    before = 0
+    for k in order:
+        z_arrival(k).wait_recv()
+        pass_on(k)
+        relay(before)
+        before = k
+    relay(before)
+    for k in range(tok_count):
+        task_copy(sibling, k, sibling, s_send, s_recv).wait_recv()
+        task_copy(flip(sibling, 2), k, sibling, r_send, r_recv).wait_recv()
+        if k:
+            z_copy(k).wait_send()
+        task_copy(task, k, partner, x_send, x_recv).wait_send()
+        task_copy(task, k, sibling, s_send, s_recv).wait_send()
+        task_copy(partner, k, sibling, r_send, r_recv).wait_send()
+
+
+def standardise(tiles, tokens):
+    sources, rows, width = tiles.shape
+    values = tiles.astype(jnp.float32)
+    count_f = jnp.sum(values[:, tokens:tokens + 1] * 16.0 + values[:, tokens + 1:tokens + 2], axis=0)
+    row = lax.broadcasted_iota(jnp.int32, (sources, rows, width), 1)
+    source = lax.broadcasted_iota(jnp.int32, (sources, rows, width), 0)
+    token = jnp.where(row < tokens, row + source * tokens, sources * rows).astype(jnp.float32)
+    live = token < count_f[None]
+    kept = jnp.where(live, values, 0.0)
+    mean = jnp.sum(jnp.sum(kept, axis=0), axis=0, keepdims=True) / count_f
+    centered = jnp.where(live, values - mean[None], 0.0)
+    variance = jnp.sum(jnp.sum(centered * centered, axis=0), axis=0, keepdims=True) / count_f
+    scaled = centered * lax.rsqrt(variance + 1e-05)[None] * lax.rsqrt(count_f)[None]
+    return scaled.astype(jnp.bfloat16).reshape(sources * rows, width)
+
+
+def tile_kernel(tokens, cand_count, buf_ref, out_ref):
+    task_count = buf_ref.shape[0]
+    width = buf_ref.shape[4]
+    step = pl.program_id(0)
+    pairs = cand_count * pl.num_programs(0)
+    task = lax.axis_index("task")
+    left = standardise(buf_ref[task, :, pairs + step], tokens)
+    for cand in range(cand_count):
+        for quarter in range(task_count):
+            right = standardise(buf_ref[quarter, :, cand_count * step + cand], tokens)
+            tile = lax.dot_general(left, right, (((0,), (0,)), ((), ())), preferred_element_type=jnp.float32)
+            out_ref[0, cand, :, quarter * width:(quarter + 1) * width] = tile.astype(jnp.bfloat16)
+
+
+def kernel_body(activations, counts, candidates):
+    tok_count = lax.axis_size("tok")
+    task_count = lax.axis_size("task")
+    tokens, blocks, width = activations.shape
+    blocks_per = counts.shape[0]
+    cand_count = candidates.shape[1]
+    pairs = blocks_per * cand_count
+    slots = pairs + blocks_per
+    held = (blocks + 15) // 16 * 16
+    tile = (slots, ROWS, width)
+    gathered = pl.pallas_call(
+        functools.partial(exchange_kernel, tok_count, blocks_per, cand_count),
+        out_shape=jax.ShapeDtypeStruct((task_count, tok_count) + tile, jnp.bfloat16),
+        in_specs=[
+            pl.BlockSpec(memory_space=pltpu.VMEM),
+            pl.BlockSpec(memory_space=pltpu.VMEM),
+            pl.BlockSpec(memory_space=pltpu.SMEM),
+        ],
+        out_specs=pl.BlockSpec(memory_space=pltpu.VMEM),
+        scratch_shapes=[
+            pltpu.VMEM((ROWS, held, width), jnp.bfloat16),
+            pltpu.VMEM((2, held, width), jnp.float32),
+            pltpu.VMEM((slots, ROWS, ROWS * held), jnp.bfloat16),
+            pltpu.VMEM((tok_count,) + tile, jnp.bfloat16),
+        ] + [pltpu.SemaphoreType.DMA((tok_count,))] * 8,
+        compiler_params=pltpu.CompilerParams(
+            collective_id=0, has_side_effects=True, vmem_limit_bytes=32 * 2**20
+        ),
+        name="exchange",
+    )(activations, counts, candidates)
+    return pl.pallas_call(
+        functools.partial(tile_kernel, tokens, cand_count),
+        grid=(blocks_per,),
+        out_shape=jax.ShapeDtypeStruct((blocks_per, cand_count, width, width * task_count), jnp.bfloat16),
+        in_specs=[pl.BlockSpec(memory_space=pltpu.VMEM)],
+        out_specs=pl.BlockSpec((1, cand_count, width, width * task_count), lambda i: (i, 0, 0, 0)),
+        compiler_params=pltpu.CompilerParams(vmem_limit_bytes=32 * 2**20),
+        name="tiles",
+    )(gathered)
+
+
 def solution(mesh):
+    small = mesh.shape["tok"] == 4 and mesh.shape["task"] == 4
     return jax.shard_map(
-        body,
+        kernel_body if small else body,
         mesh=mesh,
         in_specs=(P("tok", "layer", "task"), P(("layer", "tok"), "task"), P("layer", None)),
         out_specs=P("tok", "layer", "task", None),

time: 74.5 us -> 37.2 us (0.50)
  waiting for transfers between devices: 35.9 us -> 0 us
  Pallas kernels: 0 us -> 34.5 us
  between operations: 13.5 us -> 0.01 us
  starting transfers between devices: 9.82 us -> 0 us
  matrix products: 6.59 us -> 0 us
  other arithmetic: 4.28 us -> 0 us
  local copies, waits for them, and re-layouts: 4.02 us -> 2.4 us
    pallas_call x0 -> x2, Pallas kernels: none -> 34.5 us  [the longest x1 28.5 us: kernel_body(): pl.pallas_call(functools.partial(exchange_kernel, tok_count, blocks_per,...]
    all_gather x1 -> x0, waiting for transfers between devices: 19.3 us -> none  [body(): lax.all_gather(columns, 'task', axis=2, tiled=True)]
    all_to_all x2 -> x0, waiting for transfers between devices: 16.6 us -> none  [the longest x1 11.5 us: body(): lax.all_to_all(send_buffer, 'tok', split_axis=1, concat_axis=1, tiled=True)]
    all_to_all x2 -> x0, starting transfers between devices: 9.78 us -> none  [the longest x1 6.32 us: body(): lax.all_to_all(activations, 'tok', split_axis=1, concat_axis=0, tiled=True)]
    dot_general x1 -> x0, matrix products: 6.59 us -> none  [body(): jnp.einsum('tps,tpc->psc', rows_pair, lax.all_gather(columns, 'task', axi...]
    select_n x5 -> x0, other arithmetic: 1.77 us -> none  [the longest x1 0.9 us: body(): jnp.where((filled > 0)[None, :, None], jnp.take(scaled, picked, axis=1),...]
    gather x2 -> x0, local copies, waits for them, and re-layouts: 1.15 us -> none  [the longest x1 0.58 us: body(): jnp.take(scaled, picked, axis=1)]
    reduce_sum x4 -> x0, other arithmetic: 0.92 us -> none  [the longest x1 0.39 us: body(): rank_in = jnp.sum((same_source & earlier[None]).astype(jnp.int32), axis=2)]
  transfers between devices with their start and end apart: 3 -> 0, of which waited for: 3 -> 0; matrix products, arithmetic and copies ran while one was open for 4% -> 0% of each run, Pallas kernels for 0% -> 0%
where the time goes in v1:
time: 37.2 us; the launch traced here: 37 us
  Pallas kernels  34.5 us (93%)
  local copies, waits for them, and re-layouts  2.4 us (6%)
    pallas_call x1, Pallas kernels, kernel_body(): pl.pallas_call(functools.partial(exchange_kernel, tok_count, blocks_per,...  28.5 us
    pallas_call x1, Pallas kernels, kernel_body(): pl.pallas_call(functools.partial(tile_kernel, tokens, cand_count), grid=(...  6.06 us
    unnamed x5, local copies, waits for them, and re-layouts  2.4 us

profile of v1, /device:TPU:0, one launch (start us, length us, event | category | flops | bytes accessed | tf_op | source)
XLA Modules:
  0.0 37.0 jit_solution(2946669138252442252)
XLA Ops:
  0.0 0.8 %copy.4.cand_ref = s32[28,2]{1,0:T(8,128)S(1)} copy(s32[28,2]{0,1:T(2,128)} %param.5) | data formatting | bytes 448 | tf_op args[2]
  0.8 0.0 copy-start
  0.8 0.9 %copy-done = bf16[14,28,256]{2,1,0:T(8,128)(2,1)S(1)} copy-done((bf16[14,28,256]{2,1,0:T(8,128)(2,1)S(1)}, bf16[14,28,256]{2,1,0:T(8,128)(2,1)}, u32[]{:S(2)}) %copy-start) | copy-done | bytes 200728
  1.7 0.0 copy-start.1
  1.7 0.7 %copy-done.1 = s32[7,256]{1,0:T(8,128)S(1)} copy-done((s32[7,256]{1,0:T(8,128)S(1)}, s32[7,256]{1,0:T(8,128)}, u32[]{:S(2)}) %copy-start.1) | copy-done | bytes 7192
  2.4 28.5 %exchange.1.buf_ref = bf16[4,4,21,16,256]{4,3,2,1,0:T(8,128)(2,1)S(1)} custom-call(bf16[14,28,256]{2,1,0:T(8,128)(2,1)S(1)} %copy-done, s32[7,256]{1,0:T(8,128)S(1)} %copy-done.1, s32[28,2]{1,0:T(8,128)S(1)} %copy.4.cand_ref), custom_call_target="tpu_custom_call" | custom-call | tf_op jit(solution)/shard_map/exchange/pallas_call | solution.py:216
  30.9 6.1 %tiles.1 = bf16[7,2,256,1024]{3,2,1,0:T(8,128)(2,1)} custom-call(bf16[4,4,21,16,256]{4,3,2,1,0:T(8,128)(2,1)S(1)} %exchange.1.buf_ref), custom_call_target="tpu_custom_call" | custom-call | tf_op jit(solution)/shard_map/tiles/pallas_call | solution.py:236
Async XLA Ops:
  0.8 0.9 %copy-start = (bf16[14,28,256]{2,1,0:T(8,128)(2,1)S(1)}, bf16[14,28,256]{2,1,0:T(8,128)(2,1)}, u32[]{:S(2)}) copy-start(bf16[14,28,256]{2,1,0:T(8,128)(2,1)} %act_ref.1) | copy-start | bytes 602116
  1.7 0.7 %copy-start.1 = (s32[7,256]{1,0:T(8,128)S(1)}, s32[7,256]{1,0:T(8,128)}, u32[]{:S(2)}) copy-start(s32[7,256]{1,0:T(8,128)} %counts_ref.1) | copy-start | bytes 21508

commit v2 on v1

--- a/solution.py
+++ b/solution.py
@@ -9,6 +9,8 @@
 
 MESH = pl.DeviceIdType.MESH
 ROWS = 16
+CHUNK = 7
+ORDER = (2, 3, 1)
 
 
 def normalize(values, counts):
@@ -68,8 +70,8 @@
     return index + bit - 2 * bit * ((index // bit) % 2)
 
 
-def exchange_kernel(tok_count, blocks_per, cand_count, act_ref, counts_ref, cand_ref, out_ref,
-                    padded, count_rows, select, sending, z_send, z_recv, x_send, x_recv,
+def exchange_kernel(tok_count, blocks_per, cand_count, act_hbm, counts_hbm, cand_ref, out_ref,
+                    act_ref, counts_ref, local, padded, count_rows, select, sending, z_send, z_recv, x_send, x_recv,
                     s_send, s_recv, r_send, r_recv):
     me = lax.axis_index("tok")
     task = lax.axis_index("task")
@@ -78,6 +80,9 @@
     pairs = blocks_per * cand_count
     slots = pairs + blocks_per
     tokens, blocks, width = act_ref.shape
+    reads = [pltpu.make_async_copy(act_hbm, act_ref, local.at[0]), pltpu.make_async_copy(counts_hbm, counts_ref, local.at[1])]
+    for read in reads:
+        read.start()
     rows, held = padded.shape[0], padded.shape[1]
 
     def tok_peer(k):
@@ -95,8 +100,10 @@
         pl.semaphore_signal(barrier, inc=1, device_id={"task": other}, device_id_type=MESH)
 
     padded[...] = jnp.zeros_like(padded)
+    count_rows[...] = jnp.zeros_like(count_rows)
+    for read in reads:
+        read.wait()
     padded[0:tokens, 0:blocks, :] = act_ref[...]
-    count_rows[...] = jnp.zeros_like(count_rows)
     counts = counts_ref[...]
     for owner in range(tok_count):
         mine = jnp.where(me == owner, counts, 0)
@@ -112,7 +119,7 @@
     def pick(owner):
         for slot in range(slots):
             if slot < pairs:
-                block = cand_ref[owner * blocks_per + slot // cand_count, slot % cand_count]
+                block = cand_ref[slot % cand_count, owner * blocks_per + slot // cand_count]
             else:
                 block = owner * blocks_per + (slot - pairs)
             select[slot] = jnp.where(offset == block, 1.0, 0.0).astype(jnp.bfloat16)
@@ -121,56 +128,62 @@
         )
         return picked.astype(jnp.bfloat16).reshape(slots, rows, width)
 
-    def z_copy(k):
+    chunks = [(lo, min(lo + CHUNK, pairs)) for lo in range(0, pairs, CHUNK)] + [(pairs, slots)]
+    passed = range(len(chunks) - 1)
+
+    def z_copy(k, c, source=None):
+        lo, hi = chunks[c]
         return pltpu.make_async_remote_copy(
-            src_ref=sending.at[k], dst_ref=out_ref.at[task, me], send_sem=z_send.at[k],
-            recv_sem=z_recv.at[k], device_id={"tok": tok_peer(k)}, device_id_type=MESH)
-
-    def z_arrival(k):
+            src_ref=sending.at[k, lo:hi], dst_ref=out_ref.at[task, me if source is None else source, lo:hi],
+            send_sem=z_send.at[k, c], recv_sem=z_recv.at[k, c],
+            device_id={"tok": tok_peer(k)}, device_id_type=MESH)
+
+    def task_copy(quarter, k, c, target, send, recv):
+        lo, hi = chunks[c]
+        view = out_ref.at[quarter, tok_peer(k), lo:hi]
         return pltpu.make_async_remote_copy(
-            src_ref=sending.at[k], dst_ref=out_ref.at[task, tok_peer(k)], send_sem=z_send.at[k],
-            recv_sem=z_recv.at[k], device_id={"tok": tok_peer(k)}, device_id_type=MESH)
-
-    def task_copy(quarter, k, target, send, recv):
-        view = out_ref.at[quarter, tok_peer(k), 0:pairs]
-        return pltpu.make_async_remote_copy(
-            src_ref=view, dst_ref=view, send_sem=send.at[k],
-            recv_sem=recv.at[k], device_id={"task": target}, device_id_type=MESH)
-
-    order = [k for k in (2, 3, 1) if k < tok_count]
-    first = True
+            src_ref=view, dst_ref=view, send_sem=send.at[k, c],
+            recv_sem=recv.at[k, c], device_id={"task": target}, device_id_type=MESH)
+
+    def pass_on(k, c):
+        task_copy(task, k, c, partner, x_send, x_recv).start()
+        task_copy(task, k, c, sibling, s_send, s_recv).start()
+
+    def relay(k, c):
+        task_copy(partner, k, c, partner, x_send, x_recv).wait_recv()
+        task_copy(partner, k, c, sibling, r_send, r_recv).start()
+
+    order = [k for k in ORDER if k < tok_count]
     for k in order:
         sending[k] = pick(tok_peer(k))
-        if first:
-            pl.semaphore_wait(barrier, tok_count + 1)
-            first = False
-        z_copy(k).start()
     out_ref[task, me] = pick(me)
-
-    def pass_on(k):
-        task_copy(task, k, partner, x_send, x_recv).start()
-        task_copy(task, k, sibling, s_send, s_recv).start()
-
-    def relay(k):
-        task_copy(partner, k, partner, x_send, x_recv).wait_recv()
-        task_copy(partner, k, sibling, r_send, r_recv).start()
-
-    pass_on(0)
-    before = 0
+    pl.semaphore_wait(barrier, tok_count + 1)
+    for c in range(len(chunks)):
+        for k in order:
+            z_copy(k, c).start()
+        if c == 0:
+            for own in passed:
+                pass_on(0, own)
+    waiting = [(0, c) for c in passed]
+    for c in passed:
+        for k in order:
+            z_copy(k, c, tok_peer(k)).wait_recv()
+            pass_on(k, c)
+            waiting.append((k, c))
+            relay(*waiting.pop(0))
+    for k, c in waiting:
+        relay(k, c)
     for k in order:
-        z_arrival(k).wait_recv()
-        pass_on(k)
-        relay(before)
-        before = k
-    relay(before)
+        z_copy(k, len(chunks) - 1, tok_peer(k)).wait_recv()
+        for c in range(len(chunks)):
+            z_copy(k, c).wait_send()
     for k in range(tok_count):
-        task_copy(sibling, k, sibling, s_send, s_recv).wait_recv()
-        task_copy(flip(sibling, 2), k, sibling, r_send, r_recv).wait_recv()
-        if k:
-            z_copy(k).wait_send()
-        task_copy(task, k, partner, x_send, x_recv).wait_send()
-        task_copy(task, k, sibling, s_send, s_recv).wait_send()
-        task_copy(partner, k, sibling, r_send, r_recv).wait_send()
+        for c in passed:
+            task_copy(sibling, k, c, sibling, s_send, s_recv).wait_recv()
+            task_copy(flip(sibling, 2), k, c, sibling, r_send, r_recv).wait_recv()
+            task_copy(task, k, c, partner, x_send, x_recv).wait_send()
+            task_copy(task, k, c, sibling, s_send, s_recv).wait_send()
+            task_copy(partner, k, c, sibling, r_send, r_recv).wait_send()
 
 
 def standardise(tiles, tokens):
@@ -185,7 +198,7 @@
     mean = jnp.sum(jnp.sum(kept, axis=0), axis=0, keepdims=True) / count_f
     centered = jnp.where(live, values - mean[None], 0.0)
     variance = jnp.sum(jnp.sum(centered * centered, axis=0), axis=0, keepdims=True) / count_f
-    scaled = centered * lax.rsqrt(variance + 1e-05)[None] * lax.rsqrt(count_f)[None]
+    scaled = centered * (lax.rsqrt(variance + 1e-05) * lax.rsqrt(count_f))[None]
     return scaled.astype(jnp.bfloat16).reshape(sources * rows, width)
 
 
@@ -217,22 +230,25 @@
         functools.partial(exchange_kernel, tok_count, blocks_per, cand_count),
         out_shape=jax.ShapeDtypeStruct((task_count, tok_count) + tile, jnp.bfloat16),
         in_specs=[
-            pl.BlockSpec(memory_space=pltpu.VMEM),
-            pl.BlockSpec(memory_space=pltpu.VMEM),
+            pl.BlockSpec(memory_space=pltpu.HBM),
+            pl.BlockSpec(memory_space=pltpu.HBM),
             pl.BlockSpec(memory_space=pltpu.SMEM),
         ],
         out_specs=pl.BlockSpec(memory_space=pltpu.VMEM),
         scratch_shapes=[
+            pltpu.VMEM(activations.shape, jnp.bfloat16),
+            pltpu.VMEM(counts.shape, jnp.int32),
+            pltpu.SemaphoreType.DMA((2,)),
             pltpu.VMEM((ROWS, held, width), jnp.bfloat16),
             pltpu.VMEM((2, held, width), jnp.float32),
             pltpu.VMEM((slots, ROWS, ROWS * held), jnp.bfloat16),
             pltpu.VMEM((tok_count,) + tile, jnp.bfloat16),
-        ] + [pltpu.SemaphoreType.DMA((tok_count,))] * 8,
+        ] + [pltpu.SemaphoreType.DMA((tok_count, pairs // CHUNK + 2))] * 8,
         compiler_params=pltpu.CompilerParams(
             collective_id=0, has_side_effects=True, vmem_limit_bytes=32 * 2**20
         ),
         name="exchange",
-    )(activations, counts, candidates)
+    )(*[pltpu.with_memory_space_constraint(x, pltpu.HBM) for x in (activations, counts)], candidates.T)
     return pl.pallas_call(
         functools.partial(tile_kernel, tokens, cand_count),
         grid=(blocks_per,),

time: 37.2 us -> 32.7 us (0.88)
  Pallas kernels: 34.5 us -> 31.8 us
  local copies, waits for them, and re-layouts: 2.4 us -> 0.68 us
    pallas_call x1, Pallas kernels: 28.5 us -> 25.7 us  [kernel_body(): pl.pallas_call(functools.partial(exchange_kernel, tok_count, blocks_per,...]
    unnamed x5 -> x2, local copies, waits for them, and re-layouts: 2.4 us -> 0.68 us
where the time goes in v2:
time: 32.7 us; the launch traced here: 32.5 us
  Pallas kernels  31.8 us (97%)
  local copies, waits for them, and re-layouts  0.68 us (2%)
    pallas_call x1, Pallas kernels, kernel_body(): pl.pallas_call(functools.partial(exchange_kernel, tok_count, blocks_per,...  25.7 us
    pallas_call x1, Pallas kernels, kernel_body(): pl.pallas_call(functools.partial(tile_kernel, tokens, cand_count), grid=(...  6.08 us
    unnamed x2, local copies, waits for them, and re-layouts  0.68 us

profile of v2, /device:TPU:0, one launch (start us, length us, event | category | flops | bytes accessed | tf_op | source)
XLA Modules:
  0.0 32.5 jit_solution(5679768942540807815)
XLA Ops:
  0.0 0.0 copy-start
  0.0 0.7 %copy-done = s32[28,2]{0,1:T(2,128)S(1)} copy-done((s32[28,2]{0,1:T(2,128)S(1)}, s32[28,2]{0,1:T(2,128)}, u32[]{:S(2)}) %copy-start) | copy-done | bytes 248
  0.7 25.7 %exchange.1.buf_ref = bf16[4,4,21,16,256]{4,3,2,1,0:T(8,128)(2,1)S(1)} custom-call(bf16[14,28,256]{2,1,0:T(8,128)(2,1)} %act_hbm.1, s32[7,256]{1,0:T(8,128)} %counts_hbm.1, s32[2,28]{1,0:T(2,128)S(1)} %bitcast.1), custom_call_target="tpu_custom_call" | custom-call | tf_op jit(solution)/shard_map/exchange/pallas_call | solution.py:229
  26.4 6.1 %tiles.1 = bf16[7,2,256,1024]{3,2,1,0:T(8,128)(2,1)} custom-call(bf16[4,4,21,16,256]{4,3,2,1,0:T(8,128)(2,1)S(1)} %exchange.1.buf_ref), custom_call_target="tpu_custom_call" | custom-call | tf_op jit(solution)/shard_map/tiles/pallas_call | solution.py:252
Async XLA Ops:
  0.0 0.7 %copy-start = (s32[28,2]{0,1:T(2,128)S(1)}, s32[28,2]{0,1:T(2,128)}, u32[]{:S(2)}) copy-start(s32[28,2]{0,1:T(2,128)} %param.5) | copy-start | bytes 676

commit v3 on v2

--- a/solution.py
+++ b/solution.py
@@ -9,8 +9,10 @@
 
 MESH = pl.DeviceIdType.MESH
 ROWS = 16
-CHUNK = 7
-ORDER = (2, 3, 1)
+CHUNK = 4
+AHEAD = 2
+LAG = 1
+ORDER = (1, 2, 3)
 
 
 def normalize(values, counts):
@@ -70,8 +72,8 @@
     return index + bit - 2 * bit * ((index // bit) % 2)
 
 
-def exchange_kernel(tok_count, blocks_per, cand_count, act_hbm, counts_hbm, cand_ref, out_ref,
-                    act_ref, counts_ref, local, padded, count_rows, select, sending, z_send, z_recv, x_send, x_recv,
+def exchange_kernel(tok_count, blocks_per, cand_count, act_hbm, counts_hbm, cand_hbm, cols_ref, rows_ref,
+                    out_ref, act_ref, counts_ref, cand_ref, local, padded, count_rows, select, sending, z_send, z_recv, x_send, x_recv,
                     s_send, s_recv, r_send, r_recv):
     me = lax.axis_index("tok")
     task = lax.axis_index("task")
@@ -80,7 +82,8 @@
     pairs = blocks_per * cand_count
     slots = pairs + blocks_per
     tokens, blocks, width = act_ref.shape
-    reads = [pltpu.make_async_copy(act_hbm, act_ref, local.at[0]), pltpu.make_async_copy(counts_hbm, counts_ref, local.at[1])]
+    reads = [pltpu.make_async_copy(act_hbm, act_ref, local.at[0]), pltpu.make_async_copy(counts_hbm, counts_ref, local.at[1]),
+             pltpu.make_async_copy(cand_hbm, cand_ref, local.at[2])]
     for read in reads:
         read.start()
     rows, held = padded.shape[0], padded.shape[1]
@@ -158,29 +161,58 @@
         sending[k] = pick(tok_peer(k))
     out_ref[task, me] = pick(me)
     pl.semaphore_wait(barrier, tok_count + 1)
-    for c in range(len(chunks)):
-        for k in order:
-            z_copy(k, c).start()
-        if c == 0:
-            for own in passed:
-                pass_on(0, own)
+    for k in order:
+        z_copy(k, 0).start()
+    for own in passed:
+        pass_on(0, own)
+    for k in order:
+        z_copy(k, 1).start()
+    def finish(c):
+        for k in range(tok_count):
+            task_copy(sibling, k, c, sibling, s_send, s_recv).wait_recv()
+            task_copy(flip(sibling, 2), k, c, sibling, r_send, r_recv).wait_recv()
+
+        def one(slot, carry):
+            for quarter in range(out_ref.shape[0]):
+                cols_ref[slot, :, quarter * width:(quarter + 1) * width] = standardise(
+                    out_ref[quarter, :, slot], tokens)
+            return carry
+
+        lax.fori_loop(chunks[c][0], chunks[c][1], one, 0)
+
+    last = len(chunks) - 1
     waiting = [(0, c) for c in passed]
     for c in passed:
         for k in order:
             z_copy(k, c, tok_peer(k)).wait_recv()
+            if c + AHEAD <= last:
+                z_copy(k, c + AHEAD).start()
             pass_on(k, c)
             waiting.append((k, c))
             relay(*waiting.pop(0))
+        if c >= LAG:
+            for at in [at for at in waiting if at[1] <= c - LAG]:
+                relay(*at)
+                waiting.remove(at)
+            finish(c - LAG)
+    for k in order:
+        z_copy(k, last, tok_peer(k)).wait_recv()
     for k, c in waiting:
         relay(k, c)
-    for k in order:
-        z_copy(k, len(chunks) - 1, tok_peer(k)).wait_recv()
-        for c in range(len(chunks)):
-            z_copy(k, c).wait_send()
+
+    def one_row(slot, carry):
+        rows = standardise(out_ref[task, :, pairs + slot], tokens)
+        rows_ref[slot] = rows.astype(jnp.float32).T.astype(jnp.bfloat16)
+        return carry
+
+    lax.fori_loop(0, blocks_per, one_row, 0)
+    for c in range(max(len(passed) - LAG, 0), len(passed)):
+        finish(c)
     for k in range(tok_count):
+        if k:
+            for c in range(len(chunks)):
+                z_copy(k, c).wait_send()
         for c in passed:
-            task_copy(sibling, k, c, sibling, s_send, s_recv).wait_recv()
-            task_copy(flip(sibling, 2), k, c, sibling, r_send, r_recv).wait_recv()
             task_copy(task, k, c, partner, x_send, x_recv).wait_send()
             task_copy(task, k, c, sibling, s_send, s_recv).wait_send()
             task_copy(partner, k, c, sibling, r_send, r_recv).wait_send()
@@ -202,18 +234,20 @@
     return scaled.astype(jnp.bfloat16).reshape(sources * rows, width)
 
 
-def tile_kernel(tokens, cand_count, buf_ref, out_ref):
-    task_count = buf_ref.shape[0]
-    width = buf_ref.shape[4]
+def tile_kernel(cols_ref, rows_ref, out_ref, held, sems):
     step = pl.program_id(0)
-    pairs = cand_count * pl.num_programs(0)
-    task = lax.axis_index("task")
-    left = standardise(buf_ref[task, :, pairs + step], tokens)
+    blocks_per, cand_count = held.shape[0], held.shape[1]
+    left = rows_ref[step]
     for cand in range(cand_count):
-        for quarter in range(task_count):
-            right = standardise(buf_ref[quarter, :, cand_count * step + cand], tokens)
-            tile = lax.dot_general(left, right, (((0,), (0,)), ((), ())), preferred_element_type=jnp.float32)
-            out_ref[0, cand, :, quarter * width:(quarter + 1) * width] = tile.astype(jnp.bfloat16)
+        tile = jnp.dot(left, cols_ref[cand_count * step + cand], preferred_element_type=jnp.float32)
+        held[step, cand] = tile.astype(jnp.bfloat16)
+        pltpu.make_async_copy(held.at[step, cand], out_ref.at[step, cand], sems.at[step, cand]).start()
+
+    @pl.when(step == blocks_per - 1)
+    def _():
+        for block in range(blocks_per):
+            for cand in range(cand_count):
+                pltpu.make_async_copy(held.at[block, cand], out_ref.at[block, cand], sems.at[block, cand]).wait()
 
 
 def kernel_body(activations, counts, candidates):
@@ -226,19 +260,24 @@
     slots = pairs + blocks_per
     held = (blocks + 15) // 16 * 16
     tile = (slots, ROWS, width)
-    gathered = pl.pallas_call(
+    columns, rows = pl.pallas_call(
         functools.partial(exchange_kernel, tok_count, blocks_per, cand_count),
-        out_shape=jax.ShapeDtypeStruct((task_count, tok_count) + tile, jnp.bfloat16),
+        out_shape=(
+            jax.ShapeDtypeStruct((pairs, tok_count * ROWS, task_count * width), jnp.bfloat16),
+            jax.ShapeDtypeStruct((blocks_per, width, tok_count * ROWS), jnp.bfloat16),
+        ),
         in_specs=[
             pl.BlockSpec(memory_space=pltpu.HBM),
             pl.BlockSpec(memory_space=pltpu.HBM),
-            pl.BlockSpec(memory_space=pltpu.SMEM),
+            pl.BlockSpec(memory_space=pltpu.HBM),
         ],
-        out_specs=pl.BlockSpec(memory_space=pltpu.VMEM),
+        out_specs=(pl.BlockSpec(memory_space=pltpu.VMEM),) * 2,
         scratch_shapes=[
+            pltpu.VMEM((task_count, tok_count) + tile, jnp.bfloat16),
             pltpu.VMEM(activations.shape, jnp.bfloat16),
             pltpu.VMEM(counts.shape, jnp.int32),
-            pltpu.SemaphoreType.DMA((2,)),
+            pltpu.SMEM(candidates.shape[::-1], jnp.int32),
+            pltpu.SemaphoreType.DMA((3,)),
             pltpu.VMEM((ROWS, held, width), jnp.bfloat16),
             pltpu.VMEM((2, held, width), jnp.float32),
             pltpu.VMEM((slots, ROWS, ROWS * held), jnp.bfloat16),
@@ -248,16 +287,20 @@
             collective_id=0, has_side_effects=True, vmem_limit_bytes=32 * 2**20
         ),
         name="exchange",
-    )(*[pltpu.with_memory_space_constraint(x, pltpu.HBM) for x in (activations, counts)], candidates.T)
+    )(*[pltpu.with_memory_space_constraint(x, pltpu.HBM) for x in (activations, counts, candidates.T)])
     return pl.pallas_call(
-        functools.partial(tile_kernel, tokens, cand_count),
+        tile_kernel,
         grid=(blocks_per,),
         out_shape=jax.ShapeDtypeStruct((blocks_per, cand_count, width, width * task_count), jnp.bfloat16),
-        in_specs=[pl.BlockSpec(memory_space=pltpu.VMEM)],
-        out_specs=pl.BlockSpec((1, cand_count, width, width * task_count), lambda i: (i, 0, 0, 0)),
+        in_specs=[pl.BlockSpec(memory_space=pltpu.VMEM)] * 2,
+        out_specs=pl.BlockSpec(memory_space=pltpu.HBM),
+        scratch_shapes=[
+            pltpu.VMEM((blocks_per, cand_count, width, width * task_count), jnp.bfloat16),
+            pltpu.SemaphoreType.DMA((blocks_per, cand_count)),
+        ],
         compiler_params=pltpu.CompilerParams(vmem_limit_bytes=32 * 2**20),
         name="tiles",
-    )(gathered)
+    )(columns, rows)
 
 
 def solution(mesh):

time: 32.7 us -> 28.6 us (0.87)
  Pallas kernels: 31.8 us -> 28.5 us
  local copies, waits for them, and re-layouts: 0.68 us -> 0 us
    pallas_call x1, Pallas kernels: 6.08 us -> 3.94 us  [kernel_body(): pl.pallas_call(tile_kernel, grid=(blocks_per,), out_shape=jax.ShapeDtypeS...]
    pallas_call x1, Pallas kernels: 25.7 us -> 24.6 us  [kernel_body(): pl.pallas_call(functools.partial(exchange_kernel, tok_count, blocks_per,...]
    unnamed x2 -> x0, local copies, waits for them, and re-layouts: 0.68 us -> none
where the time goes in v3:
time: 28.6 us; the launch traced here: 28.5 us
  Pallas kernels  28.5 us (100%)
    pallas_call x1, Pallas kernels, kernel_body(): pl.pallas_call(functools.partial(exchange_kernel, tok_count, blocks_per,...  24.6 us
    pallas_call x1, Pallas kernels, kernel_body(): pl.pallas_call(tile_kernel, grid=(blocks_per,), out_shape=jax.ShapeDtypeS...  3.94 us

profile of v3, /device:TPU:0, one launch (start us, length us, event | category | flops | bytes accessed | tf_op | source)
XLA Modules:
  0.0 28.5 jit_solution(12629798151209782313)
XLA Ops:
  0.0 24.6 %exchange.1 = (bf16[14,64,1024]{2,1,0:T(8,128)(2,1)S(1)}, bf16[7,256,64]{2,1,0:T(8,128)(2,1)S(1)}) custom-call(bf16[14,28,256]{2,1,0:T(8,128)(2,1)} %act_hbm.1, s32[7,256]{1,0:T(8,128)} %counts_hbm.1, s32[2,28]{1,0:T(2,128)} %bitcast.1), custom_call_target="tpu_custom_call" | custom-call | tf_op jit(solution)/shard_map/exchange/pallas_call | solution.py:263
  24.6 3.9 %tiles.1 = bf16[7,2,256,1024]{3,2,1,0:T(8,128)(2,1)} custom-call(bf16[14,64,1024]{2,1,0:T(8,128)(2,1)S(1)} %get-tuple-element.7.cols_ref, bf16[7,256,64]{2,1,0:T(8,128)(2,1)S(1)} %get-tuple-element.8.rows_ref), custom_call_target="tpu_custom_call" | custom-call | tf_op jit(solution)/shard_map/tiles/pallas_call | solution.py:291

commit v4 on v3

--- a/solution.py
+++ b/solution.py
@@ -9,7 +9,7 @@
 
 MESH = pl.DeviceIdType.MESH
 ROWS = 16
-CHUNK = 4
+CHUNK = 7
 AHEAD = 2
 LAG = 1
 ORDER = (1, 2, 3)
@@ -161,12 +161,17 @@
         sending[k] = pick(tok_peer(k))
     out_ref[task, me] = pick(me)
     pl.semaphore_wait(barrier, tok_count + 1)
-    for k in order:
-        z_copy(k, 0).start()
     for own in passed:
+        if own == 0:
+            for k in order:
+                z_copy(k, 0).start()
         pass_on(0, own)
-    for k in order:
-        z_copy(k, 1).start()
+    for c in range(1, AHEAD):
+        for k in order:
+            z_copy(k, c).start()
+
+    token = token_ids(out_ref.shape[1], tokens, width)
+
     def finish(c):
         for k in range(tok_count):
             task_copy(sibling, k, c, sibling, s_send, s_recv).wait_recv()
@@ -175,7 +180,7 @@
         def one(slot, carry):
             for quarter in range(out_ref.shape[0]):
                 cols_ref[slot, :, quarter * width:(quarter + 1) * width] = standardise(
-                    out_ref[quarter, :, slot], tokens)
+                    out_ref[quarter, :, slot], tokens, token)
             return carry
 
         lax.fori_loop(chunks[c][0], chunks[c][1], one, 0)
@@ -201,7 +206,7 @@
         relay(k, c)
 
     def one_row(slot, carry):
-        rows = standardise(out_ref[task, :, pairs + slot], tokens)
+        rows = standardise(out_ref[task, :, pairs + slot], tokens, token)
         rows_ref[slot] = rows.astype(jnp.float32).T.astype(jnp.bfloat16)
         return carry
 
@@ -218,13 +223,16 @@
             task_copy(partner, k, c, sibling, r_send, r_recv).wait_send()
 
 
-def standardise(tiles, tokens):
+def token_ids(sources, tokens, width):
+    row = lax.broadcasted_iota(jnp.int32, (sources, ROWS, width), 1)
+    source = lax.broadcasted_iota(jnp.int32, (sources, ROWS, width), 0)
+    return jnp.where(row < tokens, row + source * tokens, sources * ROWS).astype(jnp.float32)
+
+
+def standardise(tiles, tokens, token):
     sources, rows, width = tiles.shape
     values = tiles.astype(jnp.float32)
     count_f = jnp.sum(values[:, tokens:tokens + 1] * 16.0 + values[:, tokens + 1:tokens + 2], axis=0)
-    row = lax.broadcasted_iota(jnp.int32, (sources, rows, width), 1)
-    source = lax.broadcasted_iota(jnp.int32, (sources, rows, width), 0)
-    token = jnp.where(row < tokens, row + source * tokens, sources * rows).astype(jnp.float32)
     live = token < count_f[None]
     kept = jnp.where(live, values, 0.0)
     mean = jnp.sum(jnp.sum(kept, axis=0), axis=0, keepdims=True) / count_f

time: 28.6 us -> 28.4 us (level)
  Pallas kernels: 28.5 us -> 28.1 us
    pallas_call x1, Pallas kernels: 24.6 us -> 24.2 us  [kernel_body(): pl.pallas_call(functools.partial(exchange_kernel, tok_count, blocks_per,...]
where the time goes in v4:
time: 28.4 us; the launch traced here: 28.1 us
  Pallas kernels  28.1 us (99%)
    pallas_call x1, Pallas kernels, kernel_body(): pl.pallas_call(functools.partial(exchange_kernel, tok_count, blocks_per,...  24.2 us
    pallas_call x1, Pallas kernels, kernel_body(): pl.pallas_call(tile_kernel, grid=(blocks_per,), out_shape=jax.ShapeDtypeS...  3.94 us

profile of v4, /device:TPU:0, one launch (start us, length us, event | category | flops | bytes accessed | tf_op | source)
XLA Modules:
  0.0 28.1 jit_solution(13695351223442293053)
XLA Ops:
  0.0 24.2 %exchange.1 = (bf16[14,64,1024]{2,1,0:T(8,128)(2,1)S(1)}, bf16[7,256,64]{2,1,0:T(8,128)(2,1)S(1)}) custom-call(bf16[14,28,256]{2,1,0:T(8,128)(2,1)} %act_hbm.1, s32[7,256]{1,0:T(8,128)} %counts_hbm.1, s32[2,28]{1,0:T(2,128)} %bitcast.1), custom_call_target="tpu_custom_call" | custom-call | tf_op jit(solution)/shard_map/exchange/pallas_call | solution.py:271
  24.2 3.9 %tiles.1 = bf16[7,2,256,1024]{3,2,1,0:T(8,128)(2,1)} custom-call(bf16[14,64,1024]{2,1,0:T(8,128)(2,1)S(1)} %get-tuple-element.7.cols_ref, bf16[7,256,64]{2,1,0:T(8,128)(2,1)S(1)} %get-tuple-element.8.rows_ref), custom_call_target="tpu_custom_call" | custom-call | tf_op jit(solution)/shard_map/tiles/pallas_call | solution.py:299
